TPU v7x, 32 devices: a whole 2x2x4 slice. The times are simulated.
32 devices in a mesh: packs: 2 (over x), rows: 16 (over z, y, core).
Axes of the slice: x: 2, y: 2, z: 4, core: 2. Of those that a mesh axis runs over, the one named last changes fastest.
Arguments:
- start_slab: bfloat16 [131072, 256], P(('packs', 'rows')), parts along dimension 0, may hold values from -6 to 6
- blocks: bfloat16 [1024, 8, 128, 128], P(('packs', 'rows')), parts along dimension 0
- couple: int32 [1024, 8], P(('packs', 'rows')), parts along dimension 0, may hold values from 0 to 47, as said below
- counts: int32 [1024], P(('packs', 'rows')), parts along dimension 0, may hold values from 1 to 8, as said below
- send_blocks: int32 [32, 2, 8], P(('packs', 'rows')), parts along dimension 0, may hold values from 0 to 31, as said below
- center: float32 [3], replicated, may hold values from 1.5 to 3
- halfwidth: float32 [3], replicated, may hold values from 1.5 to 3
Outputs:
- basis: float32 [131072, 256], P(('packs', 'rows')), parts along dimension 0
- projected: float32 [512, 256], P('packs'), parts along dimension 0
There are 2 independent parts, one for each index of `packs`. A program takes and returns all parts, laid end to end along the dimension named above; an argument that names none is the same for every part. Nothing has to cross between parts.
Inputs may be any that keep to these rules, and one draw needn't show every extreme that they name: couple[r, 0] is r's own local block row r mod 32; other entries are any slot. `counts`: each block row has the diagonal slot live; every device has a block row with all 8 slots live. `send_blocks`: distinct local block rows in each list.
All inputs are finite; a program needn't handle non-finite values.
Results may differ from a plain program's by a relative error of at most 0.00095.
The roundings to bfloat16 on the way count: a program that leaves them out, or rounds other values in their place, can miss the bound.
Values may be sent and summed in bfloat16 or wider, within the bound.
A program may use at most 128 MiB of HBM per device.

v0:
```python
import functools

import jax
import jax.numpy as jnp
from jax import lax
from jax.experimental import pallas as pl
from jax.experimental.pallas import tpu as pltpu
from jax.sharding import PartitionSpec as P

STEPS = 3
PANEL = 16
CHUNK = 512
F32 = jnp.float32
BF16 = jnp.bfloat16
HIGHEST = lax.Precision.HIGHEST


def filter_kernel(
    devices,
    total_rows,
    couple_ref,
    counts_ref,
    send_ref,
    center_ref,
    inverse_ref,
    start_ref,
    blocks_hbm,
    slab_out,
    sums_out,
    blocks_ref,
    own_a,
    own_b,
    ext_a,
    ext_b,
    up_a,
    up_b,
    down_a,
    down_b,
    slab_t,
    sums,
    arrived,
    total,
    load_sem,
    send_sem,
    recv_sem,
    sum_send_sem,
    sum_recv_sem,
):
    rows = blocks_ref.shape[0]
    slots = blocks_ref.shape[1]
    size = blocks_ref.shape[2]
    columns = slab_t.shape[0]
    lists = send_ref.shape[1]
    me = lax.axis_index("rows")
    levels = devices.bit_length() - 1

    def partner(level):
        distance = 1 << level
        bit = (me // distance) % 2
        return me + distance * (1 - 2 * bit), bit

    load = pltpu.make_async_copy(blocks_hbm, blocks_ref, load_sem)
    load.start()

    barrier = pltpu.get_barrier_semaphore()

    @pl.when(me > 0)
    def _():
        pl.semaphore_signal(barrier, inc=1, device_id={"rows": me - 1}, device_id_type=pl.DeviceIdType.MESH)

    @pl.when(me < devices - 1)
    def _():
        pl.semaphore_signal(barrier, inc=1, device_id={"rows": me + 1}, device_id_type=pl.DeviceIdType.MESH)

    for level in range(levels):
        pl.semaphore_signal(barrier, inc=1, device_id={"rows": partner(level)[0]}, device_id_type=pl.DeviceIdType.MESH)

    for ext in (ext_a, ext_b):
        @pl.when(me == 0)
        def _():
            ext[rows : rows + lists] = jnp.zeros((lists, size, columns), BF16)

        @pl.when(me == devices - 1)
        def _():
            ext[rows + lists : rows + 2 * lists] = jnp.zeros((lists, size, columns), BF16)

    @pl.loop(0, rows)
    def _(r):
        ext_a[r] = start_ref[r]

    ends = (me == 0).astype(jnp.int32) + (me == devices - 1).astype(jnp.int32)
    pl.semaphore_wait(barrier, levels + 2 - ends)

    def exchange(step):
        own = start_ref if step == 0 else (own_a, own_b)[step % 2]
        ext = (ext_a, ext_b)[step % 2]
        up = (up_a, up_b)[step % 2]
        down = (down_a, down_b)[step % 2]
        to_up = pltpu.make_async_remote_copy(
            src_ref=up,
            dst_ref=ext.at[pl.ds(rows, lists)],
            send_sem=send_sem.at[step, 0],
            recv_sem=recv_sem.at[step, 0],
            device_id={"rows": me + 1},
            device_id_type=pl.DeviceIdType.MESH,
        )
        to_down = pltpu.make_async_remote_copy(
            src_ref=down,
            dst_ref=ext.at[pl.ds(rows + lists, lists)],
            send_sem=send_sem.at[step, 1],
            recv_sem=recv_sem.at[step, 1],
            device_id={"rows": me - 1},
            device_id_type=pl.DeviceIdType.MESH,
        )

        def start():
            @pl.when(me < devices - 1)
            def _():
                for j in range(lists):
                    up[j] = own[send_ref[1, j]]
                to_up.start()

            @pl.when(me > 0)
            def _():
                for j in range(lists):
                    down[j] = own[send_ref[0, j]]
                to_down.start()

        def finish():
            @pl.when(me < devices - 1)
            def _():
                to_up.wait_send()
                to_down.wait_recv()

            @pl.when(me > 0)
            def _():
                to_down.wait_send()
                to_up.wait_recv()

        return start, finish

    def conduct(ext, r):
        live = counts_ref[r]
        left, right = [], []
        for k in range(slots):
            block = blocks_ref[r, k]
            left.append(jnp.where(k < live, block, jnp.zeros_like(block)))
            right.append(ext[couple_ref[r, k]])
        return jnp.dot(
            jnp.concatenate(left, axis=1), jnp.concatenate(right, axis=0), preferred_element_type=F32
        )

    for step in range(STEPS + 1):
        start, finish = exchange(step)
        start()
        ext = (ext_a, ext_b)[step % 2]
        own = start_ref if step == 0 else (own_a, own_b)[step % 2]
        if step == 0:
            load.wait()
        if step == STEPS:
            sums[...] = jnp.zeros_like(sums)
            per = CHUNK // size

            @pl.loop(0, rows // per)
            def _(c):
                part = own[pl.ds(c * per, per)].reshape(CHUNK, columns)
                part_t = part.T
                slab_t[:, pl.ds(pl.multiple_of(c * CHUNK, CHUNK), CHUNK)] = part_t
                sums[0:columns] += jnp.dot(part_t, part, preferred_element_type=F32)
                slab_out[pl.ds(c * per, per)] = own[pl.ds(c * per, per)]
        finish()
        if step < STEPS:
            own_next = (own_b, own_a)[step % 2]
            ext_next = (ext_b, ext_a)[step % 2]

            @pl.loop(0, rows)
            def _(r):
                product = conduct(ext, r)
                new = ((product - center_ref[step] * own[r].astype(F32)) * inverse_ref[step]).astype(BF16)
                own_next[r] = new
                ext_next[r] = new
        else:
            image = own_a if step % 2 else own_b

            @pl.loop(0, rows)
            def _(r):
                image[r] = conduct(ext, r).astype(BF16)

            @pl.loop(0, rows // per)
            def _(c):
                part = image[pl.ds(c * per, per)].reshape(CHUNK, columns)
                part_t = slab_t[:, pl.ds(pl.multiple_of(c * CHUNK, CHUNK), CHUNK)]
                sums[columns : 2 * columns] += jnp.dot(part_t, part, preferred_element_type=F32)

    offset = 0
    length = 2 * columns
    spans = []
    at = 0
    for level in range(levels):
        other, bit = partner(level)
        length //= 2
        keep = pl.multiple_of(offset + bit * length, length)
        give = pl.multiple_of(offset + (1 - bit) * length, length)
        copy = pltpu.make_async_remote_copy(
            src_ref=sums.at[pl.ds(give, length)],
            dst_ref=arrived.at[pl.ds(at, length)],
            send_sem=sum_send_sem.at[0, level],
            recv_sem=sum_recv_sem.at[0, level],
            device_id={"rows": other},
            device_id_type=pl.DeviceIdType.MESH,
        )
        copy.start()
        copy.wait()
        sums[pl.ds(keep, length)] += arrived[pl.ds(at, length)]
        spans.append((other, keep, length))
        offset = keep
        at += length
    total[pl.ds(offset, length)] = sums[pl.ds(offset, length)]
    for level in reversed(range(levels)):
        other, keep, length = spans[level]
        copy = pltpu.make_async_remote_copy(
            src_ref=total.at[pl.ds(keep, length)],
            dst_ref=total.at[pl.ds(keep, length)],
            send_sem=sum_send_sem.at[1, level],
            recv_sem=sum_recv_sem.at[1, level],
            device_id={"rows": other},
            device_id_type=pl.DeviceIdType.MESH,
        )
        copy.start()
        copy.wait()
    sums_out[...] = total[...] / total_rows


def invert_factor(work):
    order = work.shape[0]
    half = order // 2
    inside = lax.broadcasted_iota(jnp.int32, (PANEL, 1), 0)
    for p in range(order // PANEL):
        base, end = p * PANEL, (p + 1) * PANEL
        low = (base // half) * half
        top = low + half
        wide = work[base:end, low : order + top]
        column = [
            jnp.broadcast_to(work[base:end, base + k : base + k + 1], (PANEL, 128)) for k in range(PANEL)
        ]
        width = order + top - low
        inverse = []
        for j in range(PANEL):
            pivot = 1.0 / column[j][j : j + 1, :]
            inverse.append(pivot)
            if j < PANEL - 1:
                factor = jnp.where(inside > j, column[j] * pivot, 0.0)
                for k in range(j + 1, PANEL):
                    column[k] = column[k] - factor * column[k][j : j + 1, :]
                wide = wide - jnp.tile(factor, (1, width // 128)) * wide[j : j + 1, :]
        inverse = jnp.concatenate(inverse, axis=0)
        if end < order:
            first = (end // half) * half
            scaled = wide[:, first - low : order - low] * jnp.tile(inverse, (1, (order - first) // 128))
            ids = lax.broadcasted_iota(jnp.int32, scaled.shape, 1) + first
            scaled = jnp.where(ids >= end, scaled, 0.0)
            work[first:order, low : order + top] -= lax.dot_general(
                scaled, wide, (((0,), (0,)), ((), ())), precision=HIGHEST, preferred_element_type=F32
            )
        root = jnp.sqrt(inverse)
        work[base:end, order : order + top] = wide[:, order - low :] * jnp.tile(root, (1, top // 128))


def basis_kernel(slab_ref, sums_ref, basis_ref, projected_ref, work, high, low):
    order = slab_ref.shape[1]

    @pl.when(pl.program_id(0) == 0)
    def _():
        rows = lax.broadcasted_iota(jnp.int32, (order, order), 0)
        lanes = lax.broadcasted_iota(jnp.int32, (order, order), 1)
        work[:, 0:order] = sums_ref[0:order]
        work[:, order : 2 * order] = (rows == lanes).astype(F32)
        invert_factor(work)
        inverse = work[:, order : 2 * order]
        left = jnp.dot(inverse, sums_ref[order : 2 * order], precision=HIGHEST, preferred_element_type=F32)
        flipped = inverse.T
        projected_ref[...] = jnp.dot(left, flipped, precision=HIGHEST, preferred_element_type=F32)
        top = flipped.astype(BF16)
        high[...] = top
        low[...] = (flipped - top.astype(F32)).astype(BF16)

    slab = slab_ref[...]
    basis_ref[...] = jnp.dot(slab, high[...], preferred_element_type=F32) + jnp.dot(
        slab, low[...], preferred_element_type=F32
    )


def body(start_slab, blocks, couple, counts, send_blocks, center, halfwidth):
    rows, slots, size, _ = blocks.shape
    columns = start_slab.shape[1]
    local = start_slab.shape[0]
    lists = send_blocks.shape[2]
    devices = lax.axis_size("rows")
    total_rows = local * devices
    levels = devices.bit_length() - 1
    smem = pl.BlockSpec(memory_space=pltpu.SMEM)
    vmem = pl.BlockSpec(memory_space=pltpu.VMEM)
    own = pltpu.VMEM((rows, size, columns), BF16)
    ext = pltpu.VMEM((rows + 2 * lists, size, columns), BF16)
    listed = pltpu.VMEM((lists, size, columns), BF16)
    slab, sums = pl.pallas_call(
        functools.partial(filter_kernel, devices, float(total_rows)),
        out_shape=(
            jax.ShapeDtypeStruct((rows, size, columns), BF16),
            jax.ShapeDtypeStruct((2 * columns, columns), F32),
        ),
        in_specs=[smem] * 5 + [vmem, pl.BlockSpec(memory_space=pl.ANY)],
        out_specs=(vmem, vmem),
        scratch_shapes=[
            pltpu.VMEM(blocks.shape, BF16),
            own,
            own,
            ext,
            ext,
            listed,
            listed,
            listed,
            listed,
            pltpu.VMEM((columns, local), BF16),
            pltpu.VMEM((2 * columns, columns), F32),
            pltpu.VMEM((2 * columns, columns), F32),
            pltpu.VMEM((2 * columns, columns), F32),
            pltpu.SemaphoreType.DMA,
            pltpu.SemaphoreType.DMA((STEPS + 1, 2)),
            pltpu.SemaphoreType.DMA((STEPS + 1, 2)),
            pltpu.SemaphoreType.DMA((2, levels)),
            pltpu.SemaphoreType.DMA((2, levels)),
        ],
        compiler_params=pltpu.CompilerParams(
            collective_id=0, has_side_effects=True, vmem_limit_bytes=48 * 1024 * 1024
        ),
    )(
        couple,
        counts,
        send_blocks[0],
        center,
        1.0 / halfwidth,
        start_slab.reshape(rows, size, columns),
        blocks,
    )
    tile = 512
    return pl.pallas_call(
        basis_kernel,
        grid=(local // tile,),
        out_shape=(
            jax.ShapeDtypeStruct((local, columns), F32),
            jax.ShapeDtypeStruct((columns, columns), F32),
        ),
        in_specs=[
            pl.BlockSpec((tile, columns), lambda i: (i, 0)),
            pl.BlockSpec((2 * columns, columns), lambda i: (0, 0)),
        ],
        out_specs=(
            pl.BlockSpec((tile, columns), lambda i: (i, 0)),
            pl.BlockSpec((columns, columns), lambda i: (0, 0)),
        ),
        scratch_shapes=[
            pltpu.VMEM((columns, 2 * columns), F32),
            pltpu.VMEM((columns, columns), BF16),
            pltpu.VMEM((columns, columns), BF16),
        ],
        compiler_params=pltpu.CompilerParams(vmem_limit_bytes=32 * 1024 * 1024),
    )(slab.reshape(local, columns), sums)


def solution(mesh):
    return jax.shard_map(
        body,
        mesh=mesh,
        in_specs=(
            P(("packs", "rows"), None),
            P(("packs", "rows"), None, None, None),
            P(("packs", "rows"), None),
            P(("packs", "rows")),
            P(("packs", "rows"), None, None),
            P(),
            P(),
        ),
        out_specs=(P(("packs", "rows"), None), P("packs", None)),
        check_vma=False,
    )
```

profile of v0, /device:TPU:0, one launch (start us, length us, event | category | flops | bytes accessed | tf_op | source)
XLA Modules:
  0.0 125.5 jit_solution(3432914778148883545)
XLA Ops:
  0.6 0.7 broadcast_divide_fusion.inverse_ref
  1.3 0.8 copy.9.couple_ref
  2.1 0.0 copy-start
  2.1 1.6 %copy-done = bf16[4096,256]{1,0:T(8,128)(2,1)S(1)} copy-done((bf16[4096,256]{1,0:T(8,128)(2,1)S(1)}, bf16[4096,256]{1,0:T(8,128)(2,1)}, u32[]{:S(2)}) %copy-start) | copy-done | bytes 2097176
  3.6 0.0 copy-start.1
  3.6 0.7 copy-done.1
  4.3 0.0 copy-start.2
  4.3 0.7 copy-done.2
  5.0 0.0 copy-start.3
  5.0 0.7 copy-done.3
  5.6 102.9 %shard_map.86 = (bf16[32,128,256]{2,1,0:T(8,128)(2,1)S(1)}, f32[512,256]{1,0:T(8,128)S(1)}) custom-call(s32[32,8]{1,0:T(8,128)S(1)} %copy.9.couple_ref, s32[32]{0:T(128)S(1)} %copy-done.2, s32[2,8]{1,0:T(2,128)S(1)} %bitcast.5, f32[3]{0:T(128)S(1)} %copy-done.3, f32[3]{0:T(128)S(1)} %broadcast_divide_fusion.inverse_ref, bf16[32,128,256]{2,1,0:T(8,128)(2,1)S(1)} %bitcast.4, ...), custom_call_target="tpu_custom_call" | custom-call | tf_op jit(solution)/shard_map/pallas_call | solution.py:306
  108.6 17.0 %shard_map.87 = (f32[4096,256]{1,0:T(8,128)}, f32[256,256]{1,0:T(8,128)}) custom-call(bf16[4096,256]{1,0:T(8,128)(2,1)S(1)} %bitcast.3, f32[512,256]{1,0:T(8,128)S(1)} %get-tuple-element.5.sums_ref), custom_call_target="tpu_custom_call" | custom-call | tf_op jit(solution)/shard_map/pallas_call | solution.py:347
Async XLA Ops:
  2.1 1.6 %copy-start = (bf16[4096,256]{1,0:T(8,128)(2,1)S(1)}, bf16[4096,256]{1,0:T(8,128)(2,1)}, u32[]{:S(2)}) copy-start(bf16[4096,256]{1,0:T(8,128)(2,1)} %param.7) | copy-start | bytes 6291460
  3.6 0.7 copy-start.1
  4.3 0.7 copy-start.2
  5.0 0.7 copy-start.3
where the time goes:
time: 126 us
  Pallas kernels  120 us (95%)
  local copies, waits for them, and re-layouts  4.34 us (3%)
    pallas_call x1, Pallas kernels, body(): pl.pallas_call(functools.partial(filter_kernel, devices, float(total_rows...  103 us
    pallas_call x1, Pallas kernels, body(): pl.pallas_call(basis_kernel, grid=(local // tile,), out_shape=(jax.ShapeD...  17 us
    unnamed x9, local copies, waits for them, and re-layouts  4.34 us

commit v1 on v0

v1 whole, which is shorter than its diff:
```python
import functools

import jax
import jax.numpy as jnp
from jax import lax
from jax.experimental import pallas as pl
from jax.experimental.pallas import tpu as pltpu
from jax.sharding import PartitionSpec as P

STEPS = 3
PANEL = 16
CHUNK = 512
F32 = jnp.float32
BF16 = jnp.bfloat16
HIGHEST = lax.Precision.HIGHEST


def filter_kernel(
    devices,
    total_rows,
    table_hbm,
    scale_hbm,
    start_ref,
    blocks_hbm,
    slab_out,
    moment_out,
    inverse_out,
    high_out,
    low_out,
    blocks_ref,
    table,
    scale,
    work,
    own_a,
    own_b,
    ext_a,
    ext_b,
    up_a,
    up_b,
    down_a,
    down_b,
    slab_t,
    sums,
    arrived,
    total,
    load_sem,
    table_sem,
    send_sem,
    recv_sem,
    sum_send_sem,
    sum_recv_sem,
):
    rows = blocks_ref.shape[0]
    slots = blocks_ref.shape[1]
    size = blocks_ref.shape[2]
    columns = slab_t.shape[0]
    lists = (ext_a.shape[0] - rows) // 2
    counts_at = rows * slots
    send_at = counts_at + rows
    me = lax.axis_index("rows")
    levels = devices.bit_length() - 1

    def partner(level):
        distance = 1 << level
        bit = (me // distance) % 2
        return me + distance * (1 - 2 * bit), bit

    load = pltpu.make_async_copy(blocks_hbm, blocks_ref, load_sem)
    load.start()
    tables = (
        pltpu.make_async_copy(table_hbm, table, table_sem.at[0]),
        pltpu.make_async_copy(scale_hbm, scale, table_sem.at[1]),
    )
    for copy in tables:
        copy.start()

    barrier = pltpu.get_barrier_semaphore()

    @pl.when(me > 0)
    def _():
        pl.semaphore_signal(barrier, inc=1, device_id={"rows": me - 1}, device_id_type=pl.DeviceIdType.MESH)

    @pl.when(me < devices - 1)
    def _():
        pl.semaphore_signal(barrier, inc=1, device_id={"rows": me + 1}, device_id_type=pl.DeviceIdType.MESH)

    for level in range(levels):
        pl.semaphore_signal(barrier, inc=1, device_id={"rows": partner(level)[0]}, device_id_type=pl.DeviceIdType.MESH)

    for ext in (ext_a, ext_b):
        @pl.when(me == 0)
        def _():
            ext[rows : rows + lists] = jnp.zeros((lists, size, columns), BF16)

        @pl.when(me == devices - 1)
        def _():
            ext[rows + lists : rows + 2 * lists] = jnp.zeros((lists, size, columns), BF16)

    @pl.loop(0, rows)
    def _(r):
        ext_a[r] = start_ref[r]

    for copy in tables:
        copy.wait()
    ends = (me == 0).astype(jnp.int32) + (me == devices - 1).astype(jnp.int32)
    pl.semaphore_wait(barrier, levels + 2 - ends)

    def exchange(step):
        own = start_ref if step == 0 else (own_a, own_b)[step % 2]
        ext = (ext_a, ext_b)[step % 2]
        up = (up_a, up_b)[step % 2]
        down = (down_a, down_b)[step % 2]
        to_up = pltpu.make_async_remote_copy(
            src_ref=up,
            dst_ref=ext.at[pl.ds(rows, lists)],
            send_sem=send_sem.at[step, 0],
            recv_sem=recv_sem.at[step, 0],
            device_id={"rows": me + 1},
            device_id_type=pl.DeviceIdType.MESH,
        )
        to_down = pltpu.make_async_remote_copy(
            src_ref=down,
            dst_ref=ext.at[pl.ds(rows + lists, lists)],
            send_sem=send_sem.at[step, 1],
            recv_sem=recv_sem.at[step, 1],
            device_id={"rows": me - 1},
            device_id_type=pl.DeviceIdType.MESH,
        )

        def start():
            @pl.when(me < devices - 1)
            def _():
                for j in range(lists):
                    up[j] = own[table[send_at + lists + j]]
                to_up.start()

            @pl.when(me > 0)
            def _():
                for j in range(lists):
                    down[j] = own[table[send_at + j]]
                to_down.start()

        def finish():
            @pl.when(me < devices - 1)
            def _():
                to_up.wait_send()
                to_down.wait_recv()

            @pl.when(me > 0)
            def _():
                to_down.wait_send()
                to_up.wait_recv()

        return start, finish

    def conduct(ext, r):
        live = table[counts_at + r]
        left, right = [], []
        for k in range(slots):
            block = blocks_ref[r, k]
            left.append(jnp.where(k < live, block, jnp.zeros_like(block)))
            right.append(ext[table[r * slots + k]])
        return jnp.dot(
            jnp.concatenate(left, axis=1), jnp.concatenate(right, axis=0), preferred_element_type=F32
        )

    def reduction(which):
        phases = []
        offset = which * columns
        length = columns
        at = which * columns
        spans = []
        for level in range(levels):
            other, bit = partner(level)
            length //= 2
            keep = pl.multiple_of(offset + bit * length, length)
            give = pl.multiple_of(offset + (1 - bit) * length, length)
            copy = pltpu.make_async_remote_copy(
                src_ref=sums.at[pl.ds(give, length)],
                dst_ref=arrived.at[pl.ds(at, length)],
                send_sem=sum_send_sem.at[which, level],
                recv_sem=sum_recv_sem.at[which, level],
                device_id={"rows": other},
                device_id_type=pl.DeviceIdType.MESH,
            )

            def finish(copy=copy, keep=keep, at=at, length=length, last=level == levels - 1):
                copy.wait()
                here = pl.ds(keep, length)
                (total if last else sums)[here] = sums[here] + arrived[pl.ds(at, length)]

            phases.append((copy.start, finish))
            spans.append((other, keep, length))
            offset = keep
            at += length
        for level in reversed(range(levels)):
            other, keep, length = spans[level]
            copy = pltpu.make_async_remote_copy(
                src_ref=total.at[pl.ds(keep, length)],
                dst_ref=total.at[pl.ds(keep, length)],
                send_sem=sum_send_sem.at[which, levels + level],
                recv_sem=sum_recv_sem.at[which, levels + level],
                device_id={"rows": other},
                device_id_type=pl.DeviceIdType.MESH,
            )
            phases.append((copy.start, copy.wait))
        return phases

    for step in range(STEPS + 1):
        start, finish = exchange(step)
        start()
        ext = (ext_a, ext_b)[step % 2]
        own = start_ref if step == 0 else (own_a, own_b)[step % 2]
        if step == 0:
            load.wait()
        if step == STEPS:
            sums[...] = jnp.zeros_like(sums)
            per = CHUNK // size

            @pl.loop(0, rows // per)
            def _(c):
                part = own[pl.ds(c * per, per)].reshape(CHUNK, columns)
                part_t = part.T
                slab_t[:, pl.ds(pl.multiple_of(c * CHUNK, CHUNK), CHUNK)] = part_t
                sums[0:columns] += jnp.dot(part_t, part, preferred_element_type=F32)
                slab_out[pl.ds(c * per, per)] = own[pl.ds(c * per, per)]

            gram_phases = reduction(0)
            gram_phases[0][0]()
            gram_phases[0][1]()
            gram_phases[1][0]()
        finish()
        if step < STEPS:
            own_next = (own_b, own_a)[step % 2]
            ext_next = (ext_b, ext_a)[step % 2]

            @pl.loop(0, rows)
            def _(r):
                product = conduct(ext, r)
                new = ((product - scale[step] * own[r].astype(F32)) * scale[STEPS + step]).astype(BF16)
                own_next[r] = new
                ext_next[r] = new
        else:
            image = own_a if step % 2 else own_b

            groups = len(gram_phases) - 1
            for group in range(groups):
                @pl.loop(group * rows // groups, (group + 1) * rows // groups)
                def _(r):
                    image[r] = conduct(ext, r).astype(BF16)

                gram_phases[group + 1][1]()
                if group < groups - 1:
                    gram_phases[group + 2][0]()

            @pl.loop(0, rows // per)
            def _(c):
                part = image[pl.ds(c * per, per)].reshape(CHUNK, columns)
                part_t = slab_t[:, pl.ds(pl.multiple_of(c * CHUNK, CHUNK), CHUNK)]
                sums[columns : 2 * columns] += jnp.dot(part_t, part, preferred_element_type=F32)

    moment_phases = reduction(1)
    work[:, 0:columns] = total[0:columns] / total_rows
    ids = lax.broadcasted_iota(jnp.int32, (columns, columns), 0)
    lanes = lax.broadcasted_iota(jnp.int32, (columns, columns), 1)
    work[:, columns : 2 * columns] = (ids == lanes).astype(F32)
    panels = columns // PANEL
    done = 0
    for index, (start, finish) in enumerate(moment_phases):
        start()
        until = (index + 1) * panels // len(moment_phases)
        for p in range(done, until):
            eliminate(work, p)
        done = until
        if index == len(moment_phases) - 1:
            inverse = work[:, columns : 2 * columns]
            inverse_out[...] = inverse
            flipped = inverse.T
            top = flipped.astype(BF16)
            high_out[...] = top
            low_out[...] = (flipped - top.astype(F32)).astype(BF16)
        finish()
    moment_out[...] = total[columns : 2 * columns] / total_rows


def eliminate(work, p):
    order = work.shape[0]
    half = order // 2
    inside = lax.broadcasted_iota(jnp.int32, (PANEL, 1), 0)
    base, end = p * PANEL, (p + 1) * PANEL
    low = (base // half) * half
    top = low + half
    wide = work[base:end, low : order + top]
    column = [
        jnp.broadcast_to(work[base:end, base + k : base + k + 1], (PANEL, 128)) for k in range(PANEL)
    ]
    width = order + top - low
    inverse = []
    for j in range(PANEL):
        pivot = 1.0 / column[j][j : j + 1, :]
        inverse.append(pivot)
        if j < PANEL - 1:
            factor = jnp.where(inside > j, column[j] * pivot, 0.0)
            for k in range(j + 1, PANEL):
                column[k] = column[k] - factor * column[k][j : j + 1, :]
            wide = wide - jnp.tile(factor, (1, width // 128)) * wide[j : j + 1, :]
    inverse = jnp.concatenate(inverse, axis=0)
    if end < order:
        first = (end // half) * half
        scaled = wide[:, first - low : order - low] * jnp.tile(inverse, (1, (order - first) // 128))
        ids = lax.broadcasted_iota(jnp.int32, scaled.shape, 1) + first
        scaled = jnp.where(ids >= end, scaled, 0.0)
        work[first:order, low : order + top] -= lax.dot_general(
            scaled, wide, (((0,), (0,)), ((), ())), precision=HIGHEST, preferred_element_type=F32
        )
    root = jnp.sqrt(inverse)
    work[base:end, order : order + top] = wide[:, order - low :] * jnp.tile(root, (1, top // 128))


def basis_kernel(slab_ref, moment_ref, inverse_ref, high, low, basis_ref, projected_ref):
    @pl.when(pl.program_id(0) == pl.num_programs(0) - 1)
    def _():
        inverse = inverse_ref[...]
        left = jnp.dot(inverse, moment_ref[...], precision=HIGHEST, preferred_element_type=F32)
        projected_ref[...] = lax.dot_general(
            left, inverse, (((1,), (1,)), ((), ())), precision=HIGHEST, preferred_element_type=F32
        )

    slab = slab_ref[...]
    basis_ref[...] = jnp.dot(slab, high[...], preferred_element_type=F32) + jnp.dot(
        slab, low[...], preferred_element_type=F32
    )


def body(start_slab, blocks, couple, counts, send_blocks, center, halfwidth):
    rows, slots, size, _ = blocks.shape
    columns = start_slab.shape[1]
    local = start_slab.shape[0]
    lists = send_blocks.shape[2]
    devices = lax.axis_size("rows")
    total_rows = local * devices
    levels = devices.bit_length() - 1
    anywhere = pl.BlockSpec(memory_space=pl.ANY)
    vmem = pl.BlockSpec(memory_space=pltpu.VMEM)
    own = pltpu.VMEM((rows, size, columns), BF16)
    ext = pltpu.VMEM((rows + 2 * lists, size, columns), BF16)
    listed = pltpu.VMEM((lists, size, columns), BF16)
    table = jnp.concatenate([couple.reshape(-1), counts, send_blocks.reshape(-1)])
    scale = jnp.concatenate([center, 1.0 / halfwidth])
    square = jax.ShapeDtypeStruct((columns, columns), F32)
    half = jax.ShapeDtypeStruct((columns, columns), BF16)
    slab, moment, inverse, high, low = pl.pallas_call(
        functools.partial(filter_kernel, devices, float(total_rows)),
        out_shape=(
            jax.ShapeDtypeStruct((rows, size, columns), BF16),
            square,
            square,
            half,
            half,
        ),
        in_specs=[anywhere, anywhere, vmem, anywhere],
        out_specs=(vmem,) * 5,
        scratch_shapes=[
            pltpu.VMEM(blocks.shape, BF16),
            pltpu.SMEM(table.shape, jnp.int32),
            pltpu.SMEM(scale.shape, F32),
            pltpu.VMEM((columns, 2 * columns), F32),
            own,
            own,
            ext,
            ext,
            listed,
            listed,
            listed,
            listed,
            pltpu.VMEM((columns, local), BF16),
            pltpu.VMEM((2 * columns, columns), F32),
            pltpu.VMEM((2 * columns, columns), F32),
            pltpu.VMEM((2 * columns, columns), F32),
            pltpu.SemaphoreType.DMA,
            pltpu.SemaphoreType.DMA((2,)),
            pltpu.SemaphoreType.DMA((STEPS + 1, 2)),
            pltpu.SemaphoreType.DMA((STEPS + 1, 2)),
            pltpu.SemaphoreType.DMA((2, 2 * levels)),
            pltpu.SemaphoreType.DMA((2, 2 * levels)),
        ],
        compiler_params=pltpu.CompilerParams(
            collective_id=0, has_side_effects=True, vmem_limit_bytes=48 * 1024 * 1024
        ),
    )(
        table,
        scale,
        start_slab.reshape(rows, size, columns),
        blocks,
    )
    tile = 512
    return pl.pallas_call(
        basis_kernel,
        grid=(local // tile,),
        out_shape=(
            jax.ShapeDtypeStruct((local, columns), F32),
            jax.ShapeDtypeStruct((columns, columns), F32),
        ),
        in_specs=[
            pl.BlockSpec((tile, columns), lambda i: (i, 0)),
            *[pl.BlockSpec((columns, columns), lambda i: (0, 0))] * 4,
        ],
        out_specs=(
            pl.BlockSpec((tile, columns), lambda i: (i, 0)),
            pl.BlockSpec((columns, columns), lambda i: (0, 0)),
        ),
        compiler_params=pltpu.CompilerParams(vmem_limit_bytes=32 * 1024 * 1024),
    )(slab.reshape(local, columns), moment, inverse, high, low)


def solution(mesh):
    return jax.shard_map(
        body,
        mesh=mesh,
        in_specs=(
            P(("packs", "rows"), None),
            P(("packs", "rows"), None, None, None),
            P(("packs", "rows"), None),
            P(("packs", "rows")),
            P(("packs", "rows"), None, None),
            P(),
            P(),
        ),
        out_specs=(P(("packs", "rows"), None), P("packs", None)),
        check_vma=False,
    )
```

time: 126 us -> 130 us (1.032)
  Pallas kernels: 120 us -> 124 us
  other arithmetic: 0.66 us -> 2.12 us
    pallas_call x1, Pallas kernels: 103 us -> 118 us  [body(): pl.pallas_call(functools.partial(filter_kernel, devices, float(total_rows...]
    pallas_call x1, Pallas kernels: 17 us -> 5.71 us  [body(): pl.pallas_call(basis_kernel, grid=(local // tile,), out_shape=(jax.ShapeD...]
    unnamed x9 -> x3, local copies, waits for them, and re-layouts: 4.34 us -> 2.35 us
    concatenate x0 -> x2, other arithmetic: none -> 1.47 us  [the longest x1 0.73 us: body(): jnp.concatenate([couple.reshape(-1), counts, send_blocks.reshape(-1)])]
where the time goes in v1:
time: 130 us
  Pallas kernels  124 us (95%)
  local copies, waits for them, and re-layouts  3.2 us (2%)
  other arithmetic  2.12 us (2%)
    pallas_call x1, Pallas kernels, body(): pl.pallas_call(functools.partial(filter_kernel, devices, float(total_rows...  118 us
    pallas_call x1, Pallas kernels, body(): pl.pallas_call(basis_kernel, grid=(local // tile,), out_shape=(jax.ShapeD...  5.71 us

profile of v1, /device:TPU:0, one launch (start us, length us, event | category | flops | bytes accessed | tf_op | source)
XLA Modules:
  0.0 130.0 jit_solution(7738691624147323844)
XLA Ops:
  0.6 0.8 reshape.17
  1.4 0.7 broadcast_divide_fusion
  2.0 0.7 pad_maximum_fusion.scale_hbm
  2.8 0.8 copy.9
  3.5 0.1 reshape.16
  3.6 0.7 pad_add_fusion.table_hbm
  4.4 0.0 copy-start
  4.4 1.6 %copy-done = bf16[4096,256]{1,0:T(8,128)(2,1)S(1)} copy-done((bf16[4096,256]{1,0:T(8,128)(2,1)S(1)}, bf16[4096,256]{1,0:T(8,128)(2,1)}, u32[]{:S(2)}) %copy-start) | copy-done | bytes 2097176
  6.0 118.3 %shard_map.86 = (bf16[32,128,256]{2,1,0:T(8,128)(2,1)S(1)}, f32[256,256]{1,0:T(8,128)S(1)}, f32[256,256]{1,0:T(8,128)S(1)}, bf16[256,256]{1,0:T(8,128)(2,1)S(1)}, bf16[256,256]{1,0:T(8,128)(2,1)S(1)}) custom-call(s32[304]{0:T(512)S(1)} %pad_add_fusion.table_hbm, f32[6]{0:T(128)S(1)} %pad_maximum_fusion.scale_hbm, bf16[32,128,256]{2,1,0:T(8,128)(2,1)S(1)} %bitcast.3, ...), custom_call_target="tpu_custom_call" | custom-call | tf_op jit(solution)/shard_map/pallas_call | solution.py:352
  124.3 5.7 %shard_map.87 = (f32[4096,256]{1,0:T(8,128)}, f32[256,256]{1,0:T(8,128)}) custom-call(bf16[4096,256]{1,0:T(8,128)(2,1)S(1)} %bitcast.2, f32[256,256]{1,0:T(8,128)S(1)} %get-tuple-element.8.moment_ref, f32[256,256]{1,0:T(8,128)S(1)} %get-tuple-element.9.inverse_ref, bf16[256,256]{1,0:T(8,128)(2,1)S(1)} %get-tuple-element.10.high, ...), custom_call_target="tpu_custom_call" | custom-call | tf_op jit(solution)/shard_map/pallas_call | solution.py:397
Async XLA Ops:
  4.4 1.6 %copy-start = (bf16[4096,256]{1,0:T(8,128)(2,1)S(1)}, bf16[4096,256]{1,0:T(8,128)(2,1)}, u32[]{:S(2)}) copy-start(bf16[4096,256]{1,0:T(8,128)(2,1)} %param.7) | copy-start | bytes 6291460

commit v2 on v1

v2 whole, which is shorter than its diff:
```python
import functools

import jax
import jax.numpy as jnp
from jax import lax
from jax.experimental import pallas as pl
from jax.experimental.pallas import tpu as pltpu
from jax.sharding import PartitionSpec as P

STEPS = 3
PANEL = 16
PARTS = 2
CHUNK = 512
F32 = jnp.float32
BF16 = jnp.bfloat16
HIGHEST = lax.Precision.HIGHEST


def radices(devices):
    groups = []
    stride = 1
    while stride < devices:
        left = devices // stride
        radix = 4 if (left.bit_length() - 1) % 2 == 0 else 2
        groups.append((stride, radix))
        stride *= radix
    return groups


def filter_kernel(
    devices,
    total_rows,
    couple_hbm,
    counts_hbm,
    send_hbm,
    center_hbm,
    halfwidth_hbm,
    start_hbm,
    blocks_hbm,
    slab_out,
    moment_out,
    inverse_out,
    high_out,
    low_out,
    blocks_ref,
    couple_ref,
    counts_ref,
    send_ref,
    center_ref,
    halfwidth_ref,
    work,
    own_a,
    own_b,
    ext_0,
    ext_1,
    ext_2,
    ext_3,
    up_a,
    up_b,
    down_a,
    down_b,
    slab_t,
    sums,
    arrived,
    total,
    load_sem,
    table_sem,
    send_sem,
    recv_sem,
    sum_send_sem,
    sum_recv_sem,
):
    rows = blocks_ref.shape[0]
    slots = blocks_ref.shape[1]
    size = blocks_ref.shape[2]
    columns = slab_t.shape[0]
    exts = (ext_0, ext_1, ext_2, ext_3)
    lists = (ext_0.shape[0] - rows) // 2
    part = lists // PARTS
    me = lax.axis_index("rows")
    groups_of = radices(devices)

    def peer(stride, radix, turn):
        digit = (me // stride) % radix
        other = (digit + turn) % radix
        return me + stride * (other - digit), other

    load = pltpu.make_async_copy(blocks_hbm, blocks_ref, load_sem)
    tables = (
        pltpu.make_async_copy(start_hbm, own_a, table_sem.at[0]),
        pltpu.make_async_copy(start_hbm, ext_0.at[pl.ds(0, rows)], table_sem.at[1]),
        pltpu.make_async_copy(send_hbm, send_ref, table_sem.at[2]),
        pltpu.make_async_copy(couple_hbm, couple_ref, table_sem.at[3]),
        pltpu.make_async_copy(counts_hbm, counts_ref, table_sem.at[4]),
        pltpu.make_async_copy(center_hbm, center_ref, table_sem.at[5]),
        pltpu.make_async_copy(halfwidth_hbm, halfwidth_ref, table_sem.at[6]),
    )
    for copy in tables:
        copy.start()
    load.start()

    barrier = pltpu.get_barrier_semaphore()

    @pl.when(me > 0)
    def _():
        pl.semaphore_signal(barrier, inc=1, device_id={"rows": me - 1}, device_id_type=pl.DeviceIdType.MESH)

    @pl.when(me < devices - 1)
    def _():
        pl.semaphore_signal(barrier, inc=1, device_id={"rows": me + 1}, device_id_type=pl.DeviceIdType.MESH)

    for stride, radix in groups_of:
        for turn in range(1, radix):
            pl.semaphore_signal(
                barrier,
                inc=1,
                device_id={"rows": peer(stride, radix, turn)[0]},
                device_id_type=pl.DeviceIdType.MESH,
            )

    for ext in exts:
        @pl.when(me == 0)
        def _():
            ext[rows : rows + lists] = jnp.zeros((lists, size, columns), BF16)

        @pl.when(me == devices - 1)
        def _():
            ext[rows + lists : rows + 2 * lists] = jnp.zeros((lists, size, columns), BF16)

    for copy in tables:
        copy.wait()
    ends = (me == 0).astype(jnp.int32) + (me == devices - 1).astype(jnp.int32)
    pl.semaphore_wait(barrier, sum(radix - 1 for _, radix in groups_of) + 2 - ends)

    def exchange(step):
        ext = exts[step]
        sides = (
            ((down_a, down_b)[step % 2], rows + lists, me - 1),
            ((up_a, up_b)[step % 2], rows, me + 1),
        )
        copies = [
            [
                pltpu.make_async_remote_copy(
                    src_ref=listed.at[pl.ds(c * part, part)],
                    dst_ref=ext.at[pl.ds(first + c * part, part)],
                    send_sem=send_sem.at[step, side, c],
                    recv_sem=recv_sem.at[step, side, c],
                    device_id={"rows": target},
                    device_id_type=pl.DeviceIdType.MESH,
                )
                for c in range(PARTS)
            ]
            for side, (listed, first, target) in enumerate(sides)
        ]
        open_sides = (me > 0, me < devices - 1)

        def start(make):
            for c in range(PARTS):
                for side in (1, 0):
                    @pl.when(open_sides[side])
                    def _():
                        @pl.loop(c * part, (c + 1) * part)
                        def _(j):
                            sides[side][0][j] = make(send_ref[side, j])

                        copies[side][c].start()

        def finish():
            for side in range(2):
                @pl.when(open_sides[side])
                def _():
                    for c in range(PARTS):
                        copies[side][c].wait_send()
                        copies[1 - side][c].wait_recv()

        return start, finish

    def conduct(ext, r):
        live = counts_ref[r]
        left, right = [], []
        for k in range(slots):
            block = blocks_ref[r, k]
            left.append(jnp.where(k < live, block, jnp.zeros_like(block)))
            right.append(ext[couple_ref[k, r]])
        return jnp.dot(
            jnp.concatenate(left, axis=1), jnp.concatenate(right, axis=0), preferred_element_type=F32
        )

    def reduction(which):
        phases = []
        spans = []
        offset = which * columns
        length = columns
        at = which * columns
        flag = 0
        for index, (stride, radix) in enumerate(groups_of):
            length //= radix
            copies = []
            for turn in range(1, radix):
                other, digit = peer(stride, radix, turn)
                give = pl.multiple_of(offset + digit * length, length)
                copies.append(
                    pltpu.make_async_remote_copy(
                        src_ref=sums.at[pl.ds(give, length)],
                        dst_ref=arrived.at[pl.ds(at + (turn - 1) * length, length)],
                        send_sem=sum_send_sem.at[which, flag],
                        recv_sem=sum_recv_sem.at[which, flag],
                        device_id={"rows": other},
                        device_id_type=pl.DeviceIdType.MESH,
                    )
                )
                flag += 1
            keep = pl.multiple_of(offset + (me // stride) % radix * length, length)

            def start(copies=copies):
                for copy in copies:
                    copy.start()

            def finish(copies=copies, keep=keep, at=at, length=length, last=index == len(groups_of) - 1):
                here = sums[pl.ds(keep, length)]
                for turn, copy in enumerate(copies):
                    copy.wait()
                    here += arrived[pl.ds(at + turn * length, length)]
                (total if last else sums)[pl.ds(keep, length)] = here

            phases.append((start, finish))
            spans.append((keep, length))
            offset = keep
            at += (radix - 1) * length
        for (stride, radix), (keep, length) in zip(reversed(groups_of), reversed(spans)):
            copies = []
            for turn in range(1, radix):
                copies.append(
                    pltpu.make_async_remote_copy(
                        src_ref=total.at[pl.ds(keep, length)],
                        dst_ref=total.at[pl.ds(keep, length)],
                        send_sem=sum_send_sem.at[which, flag],
                        recv_sem=sum_recv_sem.at[which, flag],
                        device_id={"rows": peer(stride, radix, turn)[0]},
                        device_id_type=pl.DeviceIdType.MESH,
                    )
                )
                flag += 1

            def start(copies=copies):
                for copy in copies:
                    copy.start()

            def finish(copies=copies):
                for copy in copies:
                    copy.wait()

            phases.append((start, finish))
        return phases

    start, finish = exchange(0)
    start(lambda r: own_a[r])
    load.wait()
    for step in range(STEPS):
        ext, ext_next = exts[step], exts[step + 1]
        own, own_next = ((own_a, own_b), (own_b, own_a))[step % 2]
        inverse = 1.0 / jnp.full((1, columns), halfwidth_ref[step], F32)

        def apply(r):
            product = conduct(ext, r)
            return ((product - center_ref[step] * own[r].astype(F32)) * inverse).astype(BF16)

        finish()
        start, finish = exchange(step + 1)
        start(apply)

        @pl.loop(0, rows)
        def _(r):
            new = apply(r)
            own_next[r] = new
            ext_next[r] = new

    own, image = ((own_a, own_b), (own_b, own_a))[STEPS % 2]
    ext = exts[STEPS]
    sums[...] = jnp.zeros_like(sums)
    per = CHUNK // size

    @pl.loop(0, rows // per)
    def _(c):
        part = own[pl.ds(c * per, per)].reshape(CHUNK, columns)
        part_t = part.T
        slab_t[:, pl.ds(pl.multiple_of(c * CHUNK, CHUNK), CHUNK)] = part_t
        sums[0:columns] += jnp.dot(part_t, part, preferred_element_type=F32)
        slab_out[pl.ds(c * per, per)] = own[pl.ds(c * per, per)]

    gram_phases = reduction(0)
    gram_phases[0][0]()
    gram_phases[0][1]()
    gram_phases[1][0]()
    finish()
    groups = len(gram_phases) - 1
    for group in range(groups):
        @pl.loop(group * rows // groups, (group + 1) * rows // groups)
        def _(r):
            image[r] = conduct(ext, r).astype(BF16)

        gram_phases[group + 1][1]()
        if group < groups - 1:
            gram_phases[group + 2][0]()

    @pl.loop(0, rows // per)
    def _(c):
        part = image[pl.ds(c * per, per)].reshape(CHUNK, columns)
        part_t = slab_t[:, pl.ds(pl.multiple_of(c * CHUNK, CHUNK), CHUNK)]
        sums[columns : 2 * columns] += jnp.dot(part_t, part, preferred_element_type=F32)

    moment_phases = reduction(1)
    work[:, 0:columns] = total[0:columns] / total_rows
    ids = lax.broadcasted_iota(jnp.int32, (columns, columns), 0)
    lanes = lax.broadcasted_iota(jnp.int32, (columns, columns), 1)
    work[:, columns : 2 * columns] = (ids == lanes).astype(F32)
    panels = columns // PANEL
    done = 0
    for index, (start, finish) in enumerate(moment_phases):
        start()
        until = (index + 1) * panels // len(moment_phases)
        for p in range(done, until):
            pl.when(me >= 0)(functools.partial(eliminate, work, p))
        done = until
        if index == len(moment_phases) - 1:
            inverse = work[:, columns : 2 * columns]
            inverse_out[...] = inverse
            flipped = inverse.T
            top = flipped.astype(BF16)
            high_out[...] = top
            low_out[...] = (flipped - top.astype(F32)).astype(BF16)
        finish()
    moment_out[...] = total[columns : 2 * columns] / total_rows


def eliminate(work, p):
    order = work.shape[0]
    half = order // 2
    inside = lax.broadcasted_iota(jnp.int32, (PANEL, 1), 0)
    base, end = p * PANEL, (p + 1) * PANEL
    low = (base // half) * half
    top = low + half
    wide = work[base:end, low : order + top]
    column = [
        jnp.broadcast_to(work[base:end, base + k : base + k + 1], (PANEL, 128)) for k in range(PANEL)
    ]
    width = order + top - low
    inverse = []
    for j in range(PANEL):
        pivot = 1.0 / column[j][j : j + 1, :]
        inverse.append(pivot)
        if j < PANEL - 1:
            factor = jnp.where(inside > j, column[j] * pivot, 0.0)
            for k in range(j + 1, PANEL):
                column[k] = column[k] - factor * column[k][j : j + 1, :]
            wide = wide - jnp.tile(factor, (1, width // 128)) * wide[j : j + 1, :]
    inverse = jnp.concatenate(inverse, axis=0)
    if end < order:
        first = (end // half) * half
        scaled = wide[:, first - low : order - low] * jnp.tile(inverse, (1, (order - first) // 128))
        ids = lax.broadcasted_iota(jnp.int32, scaled.shape, 1) + first
        scaled = jnp.where(ids >= end, scaled, 0.0)
        work[first:order, low : order + top] -= lax.dot_general(
            scaled, wide, (((0,), (0,)), ((), ())), precision=HIGHEST, preferred_element_type=F32
        )
    root = jnp.sqrt(inverse)
    work[base:end, order : order + top] = wide[:, order - low :] * jnp.tile(root, (1, top // 128))


def basis_kernel(slab_ref, moment_ref, inverse_ref, high, low, basis_ref, projected_ref):
    @pl.when(pl.program_id(0) == pl.num_programs(0) - 1)
    def _():
        inverse = inverse_ref[...]
        left = jnp.dot(inverse, moment_ref[...], precision=HIGHEST, preferred_element_type=F32)
        projected_ref[...] = lax.dot_general(
            left, inverse, (((1,), (1,)), ((), ())), precision=HIGHEST, preferred_element_type=F32
        )

    slab = slab_ref[...]
    basis_ref[...] = jnp.dot(slab, high[...], preferred_element_type=F32) + jnp.dot(
        slab, low[...], preferred_element_type=F32
    )


def body(start_slab, blocks, couple, counts, send_blocks, center, halfwidth):
    rows, slots, size, _ = blocks.shape
    columns = start_slab.shape[1]
    local = start_slab.shape[0]
    lists = send_blocks.shape[2]
    devices = lax.axis_size("rows")
    total_rows = local * devices
    flags = 2 * sum(radix - 1 for _, radix in radices(devices))
    anywhere = pl.BlockSpec(memory_space=pltpu.HBM)
    vmem = pl.BlockSpec(memory_space=pltpu.VMEM)
    own = pltpu.VMEM((rows, size, columns), BF16)
    ext = pltpu.VMEM((rows + 2 * lists, size, columns), BF16)
    listed = pltpu.VMEM((lists, size, columns), BF16)
    square = jax.ShapeDtypeStruct((columns, columns), F32)
    half = jax.ShapeDtypeStruct((columns, columns), BF16)
    slab, moment, inverse, high, low = pl.pallas_call(
        functools.partial(filter_kernel, devices, float(total_rows)),
        out_shape=(
            jax.ShapeDtypeStruct((rows, size, columns), BF16),
            square,
            square,
            half,
            half,
        ),
        in_specs=[anywhere] * 7,
        out_specs=(vmem,) * 5,
        scratch_shapes=[
            pltpu.VMEM(blocks.shape, BF16),
            pltpu.SMEM((slots, rows), jnp.int32),
            pltpu.SMEM((rows,), jnp.int32),
            pltpu.SMEM((2, lists), jnp.int32),
            pltpu.SMEM((STEPS,), F32),
            pltpu.SMEM((STEPS,), F32),
            pltpu.VMEM((columns, 2 * columns), F32),
            own,
            own,
            *[ext] * (STEPS + 1),
            listed,
            listed,
            listed,
            listed,
            pltpu.VMEM((columns, local), BF16),
            pltpu.VMEM((2 * columns, columns), F32),
            pltpu.VMEM((2 * columns, columns), F32),
            pltpu.VMEM((2 * columns, columns), F32),
            pltpu.SemaphoreType.DMA,
            pltpu.SemaphoreType.DMA((7,)),
            pltpu.SemaphoreType.DMA((STEPS + 1, 2, PARTS)),
            pltpu.SemaphoreType.DMA((STEPS + 1, 2, PARTS)),
            pltpu.SemaphoreType.DMA((2, flags)),
            pltpu.SemaphoreType.DMA((2, flags)),
        ],
        compiler_params=pltpu.CompilerParams(
            collective_id=0, has_side_effects=True, vmem_limit_bytes=48 * 1024 * 1024
        ),
    )(
        couple.T,
        counts,
        send_blocks[0],
        center,
        halfwidth,
        start_slab.reshape(rows, size, columns),
        blocks,
    )
    tile = 512
    return pl.pallas_call(
        basis_kernel,
        grid=(local // tile,),
        out_shape=(
            jax.ShapeDtypeStruct((local, columns), F32),
            jax.ShapeDtypeStruct((columns, columns), F32),
        ),
        in_specs=[
            pl.BlockSpec((tile, columns), lambda i: (i, 0)),
            *[pl.BlockSpec((columns, columns), lambda i: (0, 0))] * 4,
        ],
        out_specs=(
            pl.BlockSpec((tile, columns), lambda i: (i, 0)),
            pl.BlockSpec((columns, columns), lambda i: (0, 0)),
        ),
        compiler_params=pltpu.CompilerParams(vmem_limit_bytes=32 * 1024 * 1024),
    )(slab.reshape(local, columns), moment, inverse, high, low)


def solution(mesh):
    return jax.shard_map(
        body,
        mesh=mesh,
        in_specs=(
            P(("packs", "rows"), None),
            P(("packs", "rows"), None, None, None),
            P(("packs", "rows"), None),
            P(("packs", "rows")),
            P(("packs", "rows"), None, None),
            P(),
            P(),
        ),
        out_specs=(P(("packs", "rows"), None), P("packs", None)),
        check_vma=False,
    )
```

time: 130 us -> 110 us (0.85)
  Pallas kernels: 124 us -> 104 us
  other arithmetic: 2.12 us -> 0 us
  local copies, waits for them, and re-layouts: 3.2 us -> 4.91 us
    pallas_call x1, Pallas kernels: 118 us -> 98.5 us  [body(): pl.pallas_call(functools.partial(filter_kernel, devices, float(total_rows...]
    unnamed x3 -> x12, local copies, waits for them, and re-layouts: 2.35 us -> 4.91 us
    concatenate x2 -> x0, other arithmetic: 1.47 us -> none  [the longest x1 0.73 us: body(): jnp.concatenate([couple.reshape(-1), counts, send_blocks.reshape(-1)])]
where the time goes in v2:
time: 110 us
  Pallas kernels  104 us (95%)
  local copies, waits for them, and re-layouts  4.91 us (4%)
    pallas_call x1, Pallas kernels, body(): pl.pallas_call(functools.partial(filter_kernel, devices, float(total_rows...  98.5 us
    pallas_call x1, Pallas kernels, body(): pl.pallas_call(basis_kernel, grid=(local // tile,), out_shape=(jax.ShapeD...  5.7 us
    unnamed x12, local copies, waits for them, and re-layouts  4.91 us

profile of v2, /device:TPU:0, one launch (start us, length us, event | category | flops | bytes accessed | tf_op | source)
XLA Modules:
  0.0 109.7 jit_solution(17672088389127613691)
XLA Ops:
  0.6 0.0 copy-start
  0.6 1.6 %copy-done = bf16[4096,256]{1,0:T(8,128)(2,1)S(1)} copy-done((bf16[4096,256]{1,0:T(8,128)(2,1)S(1)}, bf16[4096,256]{1,0:T(8,128)(2,1)}, u32[]{:S(2)}) %copy-start) | copy-done | bytes 2097176
  2.2 0.0 copy-start.1
  2.2 0.7 copy-done.1
  2.9 0.0 copy-start.2
  2.9 0.7 copy-done.2
  3.6 0.0 copy-start.3
  3.6 0.7 copy-done.3
  4.2 0.0 copy-start.4
  4.2 0.7 copy-done.4
  4.9 0.0 copy-start.5
  4.9 0.7 copy-done.5
  5.6 98.5 %shard_map.86 = (bf16[32,128,256]{2,1,0:T(8,128)(2,1)S(1)}, f32[256,256]{1,0:T(8,128)S(1)}, f32[256,256]{1,0:T(8,128)S(1)}, bf16[256,256]{1,0:T(8,128)(2,1)S(1)}, bf16[256,256]{1,0:T(8,128)(2,1)S(1)}) custom-call(s32[8,32]{1,0:T(8,128)S(1)} %bitcast.6, s32[32]{0:T(128)S(1)} %copy-done.3, s32[2,8]{1,0:T(2,128)S(1)} %bitcast.7, f32[3]{0:T(128)S(1)} %copy-done.4, ...), custom_call_target="tpu_custom_call" | custom-call | tf_op jit(solution)/shard_map/pallas_call | solution.py:400
  104.0 5.7 %shard_map.87 = (f32[4096,256]{1,0:T(8,128)}, f32[256,256]{1,0:T(8,128)}) custom-call(bf16[4096,256]{1,0:T(8,128)(2,1)S(1)} %bitcast.4, f32[256,256]{1,0:T(8,128)S(1)} %get-tuple-element.8.moment_ref, f32[256,256]{1,0:T(8,128)S(1)} %get-tuple-element.9.inverse_ref, bf16[256,256]{1,0:T(8,128)(2,1)S(1)} %get-tuple-element.10.high, ...), custom_call_target="tpu_custom_call" | custom-call | tf_op jit(solution)/shard_map/pallas_call | solution.py:450
Async XLA Ops:
  0.6 1.6 %copy-start = (bf16[4096,256]{1,0:T(8,128)(2,1)S(1)}, bf16[4096,256]{1,0:T(8,128)(2,1)}, u32[]{:S(2)}) copy-start(bf16[4096,256]{1,0:T(8,128)(2,1)} %param.7) | copy-start | bytes 6291460
  2.2 0.7 copy-start.1
  2.9 0.7 copy-start.2
  3.6 0.7 copy-start.3
  4.2 0.7 copy-start.4
  4.9 0.7 copy-start.5
